TPU v7x, 32 devices: a whole 2x2x4 slice. The times are simulated.
32 devices in a mesh: dp: 4 (over y, x), tensor: 8 (over z, core).
Axes of the slice: x: 2, y: 2, z: 4, core: 2. Of those that a mesh axis runs over, the one named last changes fastest.
Arguments:
- tokens: bfloat16 [1024, 8192], P('dp'), may hold values from -6 to 6
- out_grad: bfloat16 [1024, 8192], P('dp'), may hold values from -6 to 6
- weight_tiles: bfloat16 [256, 2, 3, 128, 128], P(('dp', 'tensor')), may hold values from -0.125 to 0.125
- tile_places: int32 [256, 2], P(('dp', 'tensor')), may hold values from 0 to 1663, as said below
- live_counts: int32 [256], P(('dp', 'tensor')), may hold values from 0 to 2, as said below
Outputs:
- layer_out: bfloat16 [1024, 8192], P('dp', 'tensor')
- input_grad: bfloat16 [1024, 8192], P('dp', 'tensor')
Inputs may be any that keep to these rules, and one draw needn't show every extreme that they name: `tile_places`: among the slots addressed to one owner, live or not, no two have the same place; the place 64 * 26 - 1 occurs in a live slot of every owner. `live_counts`: every owner receives 2 live slots from some source, and some owner receives 2 live slots from every source; slots past the count hold padding.
All inputs are finite; a program needn't handle non-finite values.
Results may differ from a plain program's by a relative error of at most 0.012.
Values may be sent and summed in bfloat16 or wider, within the bound.
A program may use at most 192 MiB of HBM per device.

v0:
```python
import jax
import jax.numpy as jnp
from jax import lax
from jax.sharding import PartitionSpec as P

FF = 26624


def block_length(extent):
    length = min(extent, 32)
    while extent % length:
        length -= 1
    return length


def over_blocks(step, running, arrays):
    extent = arrays[0].shape[0]
    length = block_length(extent)
    shaped = tuple((item.reshape((extent // length, length) + item.shape[1:]) for item in arrays))

    def advance(acc_value, slot_block):
        return (step(acc_value, slot_block), None)

    running, _ = lax.scan(advance, running, shaped)
    return running


def body(tokens, out_grad, weight_tiles, tile_places, live_counts):
    tok_rows = tokens.shape[0]
    feat_width = tokens.shape[1]
    tile_side = weight_tiles.shape[-1]
    peer_slots = weight_tiles.shape[1]
    row_count = feat_width // tile_side
    owners = lax.axis_size("tensor")
    col_count = FF // (tile_side * owners)
    arrived_tiles, arrived_places, arrived_counts = (
        lax.all_to_all(weight_tiles, "tensor", split_axis=0, concat_axis=0, tiled=True),
        lax.all_to_all(tile_places, "tensor", split_axis=0, concat_axis=0, tiled=True),
        lax.all_to_all(live_counts, "tensor", split_axis=0, concat_axis=0, tiled=True),
    )
    slot_tiles, slot_places, slot_counts = (
        lax.all_gather(arrived_tiles, "dp", axis=0, tiled=True),
        lax.all_gather(arrived_places, "dp", axis=0, tiled=True),
        lax.all_gather(arrived_counts, "dp", axis=0, tiled=True),
    )
    slot_total = slot_places.shape[0] * peer_slots
    row_ids = (slot_places // col_count).reshape(-1).astype(jnp.int32)
    col_ids = (slot_places % col_count).reshape(-1).astype(jnp.int32)
    live_mask = (jnp.arange(peer_slots)[None, :] < slot_counts[:, None]).reshape(-1)
    flat_tiles = slot_tiles.reshape((slot_total,) + slot_tiles.shape[2:])
    flat_tiles = jnp.where(
        live_mask[:, None, None, None], flat_tiles, jnp.zeros((), flat_tiles.dtype)
    )
    slot_data = (flat_tiles, row_ids, col_ids)
    token_blocks = tokens.reshape(tok_rows, row_count, tile_side)

    def gate_up_step(acc_value, slot_block):
        weights, row_block, col_block = slot_block
        gathered = jnp.take(token_blocks, row_block, axis=1)
        products = jnp.einsum(
            "tsa,sgab->gtsb", gathered, weights[:, 0:2], preferred_element_type=jnp.float32
        )
        return acc_value.at[:, :, col_block, :].add(products)

    preact = over_blocks(
        gate_up_step, jnp.zeros((2, tok_rows, col_count, tile_side), jnp.float32), slot_data
    )
    gate_pre = preact[0]
    up_pre = preact[1]
    sigmoid_gate = jax.nn.sigmoid(gate_pre)
    gate_act = gate_pre * sigmoid_gate
    hidden = (gate_act * up_pre).astype(jnp.bfloat16)

    def down_step(acc_value, slot_block):
        weights, row_block, col_block = slot_block
        gathered = jnp.take(hidden, col_block, axis=1)
        products = jnp.einsum(
            "tsa,sab->tsb", gathered, weights[:, 2], preferred_element_type=jnp.float32
        )
        return acc_value.at[:, row_block, :].add(products)

    out_part = over_blocks(
        down_step, jnp.zeros((tok_rows, row_count, tile_side), jnp.float32), slot_data
    ).reshape(tok_rows, feat_width)
    layer_out = lax.psum_scatter(
        out_part.astype(jnp.bfloat16), "tensor", scatter_dimension=1, tiled=True
    )
    grad_blocks = out_grad.reshape(tok_rows, row_count, tile_side)

    def back_step(acc_value, slot_block):
        weights, row_block, col_block = slot_block
        gathered = jnp.take(grad_blocks, row_block, axis=1)
        products = jnp.einsum(
            "tsb,sab->tsa", gathered, weights[:, 2], preferred_element_type=jnp.float32
        )
        return acc_value.at[:, col_block, :].add(products)

    grad_hidden = over_blocks(
        back_step, jnp.zeros((tok_rows, col_count, tile_side), jnp.float32), slot_data
    )
    grad_gate = (
        grad_hidden * up_pre * (sigmoid_gate * (1.0 + gate_pre * (1.0 - sigmoid_gate)))
    ).astype(jnp.bfloat16)
    grad_up = (grad_hidden * gate_act).astype(jnp.bfloat16)
    grad_pair = jnp.stack([grad_gate, grad_up])

    def input_step(acc_value, slot_block):
        weights, row_block, col_block = slot_block
        gathered = jnp.take(grad_pair, col_block, axis=2)
        products = jnp.einsum(
            "gtsb,sgab->tsa", gathered, weights[:, 0:2], preferred_element_type=jnp.float32
        )
        return acc_value.at[:, row_block, :].add(products)

    in_part = over_blocks(
        input_step, jnp.zeros((tok_rows, row_count, tile_side), jnp.float32), slot_data
    ).reshape(tok_rows, feat_width)
    input_grad = lax.psum_scatter(
        in_part.astype(jnp.bfloat16), "tensor", scatter_dimension=1, tiled=True
    )
    return (layer_out, input_grad)


def solution(mesh):
    in_specs = (
        P("dp", None),
        P("dp", None),
        P(("dp", "tensor"), None, None, None, None),
        P(("dp", "tensor"), None),
        P(("dp", "tensor")),
    )
    out_specs = (P("dp", "tensor"), P("dp", "tensor"))
    return jax.shard_map(body, mesh=mesh, in_specs=in_specs, out_specs=out_specs, check_vma=False)
```

profile of v0, /device:TPU:10, one launch (start us, length us, event | category | flops | bytes accessed | tf_op | source)
XLA Modules:
  0.0 399.5 jit_solution(2578205139297796959)
XLA Ops:
  7.2 40.9 %all_to_all.29 = bf16[8,2,3,128,128]{4,3,2,1,0:T(8,128)(2,1)} all-to-all(bf16[8,2,3,128,128]{4,3,2,1,0:T(8,128)(2,1)} %param.17), channel_id=1, replica_groups=mesh['dp'=4,'tensor'=8] {'tensor'}, dimensions={0} | all-to-all | bytes 3145728 | tf_op jit(solution)/shard_map/all_to_all | solution.py:37
  48.8 5.6 %all-to-all-start.1 = ((s32[8,1,1]{2,1,0:T(1,128)}), s32[8,1,1]{2,1,0:T(1,128)S(1)}, u32[]{:S(2)}, u32[]{:S(2)}) async-start(s32[8,1,1]{2,1,0:T(1,128)} %copy.83), calls=%async_computation.1 | async-start | bytes 8192 | tf_op jit(solution)/shard_map/all_to_all | solution.py:39
  55.2 6.6 %copy.90 = bf16[256,8192]{0,1:T(8,128)(2,1)} copy(bf16[256,8192]{1,0:T(8,128)(2,1)} %param.16) | data formatting | bytes 8388608 | tf_op args[1]
  61.8 6.4 %copy.92 = bf16[256,64,128]{2,0,1:T(8,128)(2,1)} copy(bf16[256,64,128]{0,2,1:T(8,128)(2,1)} %bitcast.209) | data formatting | bytes 8388608 | tf_op jit(solution)/shard_map/while | solution.py:24
  68.2 6.4 %copy.85 = bf16[256,8192]{0,1:T(8,128)(2,1)} copy(bf16[256,8192]{1,0:T(8,128)(2,1)} %param.15) | data formatting | bytes 8388608 | tf_op args[0]
  74.6 6.4 %copy.87 = bf16[256,64,128]{2,0,1:T(8,128)(2,1)} copy(bf16[256,64,128]{0,2,1:T(8,128)(2,1)} %bitcast.210) | data formatting | bytes 8388608 | tf_op jit(solution)/shard_map/while | solution.py:24
  82.3 5.1 %all-to-all-start = ((s32[8,1,2]{2,1,0:T(1,128)}), s32[8,1,2]{2,1,0:T(1,128)S(1)}, u32[]{:S(2)}, u32[]{:S(2)}) async-start(s32[8,1,2]{2,1,0:T(1,128)} %copy.78), calls=%async_computation | async-start | bytes 8192 | tf_op jit(solution)/shard_map/all_to_all | solution.py:38
  87.9 7.5 %all-reduce = s32[32]{0:T(128)S(1)} all-reduce(s32[32]{0:T(128)S(1)} %dynamic-update-slice), channel_id=3, replica_groups=mesh['dp'=4,'tensor'=8] {'dp'}, use_global_device_ids=true, to_apply=%add | all-reduce | flops 32 | bytes 256
  95.6 7.4 %all-gather = s32[32,1,2]{2,1,0:T(1,128)S(1)} all-gather(s32[8,1,2]{2,1,0:T(1,128)S(1)} %all-to-all-done), channel_id=2, replica_groups=mesh['dp'=4,'tensor'=8] {'dp'}, dimensions={0}, use_global_device_ids=true | all-gather | bytes 320 | tf_op jit(solution)/shard_map/all_gather | solution.py:43
  103.5 15.9 %all-gather.4.cloned.1.call-done = bf16[32,2,3,128,128]{4,3,2,1,0:T(8,128)(2,1)} async-done(((bf16[8,2,3,128,128]{4,3,2,1,0:T(8,128)(2,1)}), bf16[32,2,3,128,128]{4,3,2,1,0:T(8,128)(2,1)}) %all-gather.4.cloned.1.call-update) | async-done | bytes 6291472 | tf_op jit(solution)/shard_map/all_gather | solution.py:42
  119.4 3.3 bitcast_select_fusion
  122.6 4.5 %copy.88 = bf16[2,32,3,128,128]{4,3,1,2,0:T(8,128)(2,1)} copy(bf16[2,32,3,128,128]{4,3,2,1,0:T(8,128)(2,1)S(1)} %bitcast_select_fusion) | data formatting | bytes 12582912 | tf_op jit(solution)/shard_map/while | solution.py:24
  127.5 32.4 %while.42 = (s32[]{:T(128)}, f32[256,26,128]{2,0,1:T(8,128)S(1)}, s32[2,32]{1,0:T(2,128)S(1)}, bf16[2,32,3,128,128]{4,3,1,2,0:T(8,128)(2,1)}, s32[2,32]{1,0:T(2,...) while((s32[]{:T(128)}, f32[256,26,128]{2,0,1:T(8,128)S(1)}, s32[2,32]{1,0:T(2,128)S(1)}, ...), condition=%wide.region_9.11_spmd, body=%wide.region_7.10_spmd.sunk | while | flops 270533920 | bytes 38802964 | solution.py:24
  127.7 4.3 %gather_fusion.2 = bf16[32,256,128]{2,1,0:T(8,128)(2,1)} fusion(bf16[256,64,128]{2,0,1:T(8,128)(2,1)} %get-tuple-element.508, s32[1024]{0:T(1024)S(1)} %pad_clamp_fusion.10), kind=kCustom, calls=%fused_computation.3.clone.clone.1 | custom fusion | bytes 4194432 | tf_op jit(solution)/shard_map/while/body/eval_jaxpr/jit(_take)/gather | solution.py:92
  132.1 2.4 dynamic-slice_bitcast_fusion.7
  134.6 2.7 fusion.74
  137.3 6.5 %scatter_fusion.2 = f32[256,26,128]{2,0,1:T(8,128)S(1)} fusion(f32[256,26,128]{2,0,1:T(8,128)S(1)} %get-tuple-element.497, s32[32]{0:T(128)S(1)} %fusion.73, f32[32,256,128]{2,1,0:T(8,128)} %fusion.74), kind=kCustom, calls=%fused_computation.7.clone.1 | custom fusion | flops 1048576 | bytes 12583040 | tf_op jit(solution)/shard_map/while/body/eval_jaxpr/scatter-add | solution.py:96
  143.9 4.3 %gather_fusion.2 = bf16[32,256,128]{2,1,0:T(8,128)(2,1)} fusion(bf16[256,64,128]{2,0,1:T(8,128)(2,1)} %get-tuple-element.508, s32[1024]{0:T(1024)S(1)} %pad_clamp_fusion.10), kind=kCustom, calls=%fused_computation.3.clone.clone.1 | custom fusion | bytes 4194432 | tf_op jit(solution)/shard_map/while/body/eval_jaxpr/jit(_take)/gather | solution.py:92
  150.8 2.7 fusion.74
  153.5 6.5 %scatter_fusion.2 = f32[256,26,128]{2,0,1:T(8,128)S(1)} fusion(f32[256,26,128]{2,0,1:T(8,128)S(1)} %get-tuple-element.497, s32[32]{0:T(128)S(1)} %fusion.73, f32[32,256,128]{2,1,0:T(8,128)} %fusion.74), kind=kCustom, calls=%fused_computation.7.clone.1 | custom fusion | flops 1048576 | bytes 12583040 | tf_op jit(solution)/shard_map/while/body/eval_jaxpr/scatter-add | solution.py:96
  160.0 3.6 broadcast_in_dim.55
  163.6 77.4 %while.40 = (s32[]{:T(128)}, f32[2,256,26,128]{3,1,2,0:T(8,128)}, s32[2,32]{1,0:T(2,128)S(1)}, bf16[2,32,3,128,128]{4,3,2,1,0:T(8,128)(2,1)}, s32[2,32]{1,0:T(2,...) while((s32[]{:T(128)}, f32[2,256,26,128]{3,1,2,0:T(8,128)}, s32[2,32]{1,0:T(2,128)S(1)}, ...), condition=%wide.region_2.4_spmd, body=%wide.region_0.3_spmd.sunk | while | flops 540017984 | bytes 59774484 | solution.py:24
  163.6 4.3 %gather_fusion = bf16[32,256,128]{2,1,0:T(8,128)(2,1)} fusion(bf16[256,64,128]{2,0,1:T(8,128)(2,1)} %get-tuple-element.487, s32[1024]{0:T(1024)S(1)} %pad_clamp_fusion.8), kind=kCustom, calls=%fused_computation.clone.clone.1 | custom fusion | bytes 4194432 | tf_op jit(solution)/shard_map/while/body/eval_jaxpr/jit(_take)/gather | solution.py:59
  167.9 6.8 %convolution_bitcast_fusion.2 = f32[32,2,256,128]{2,3,1,0:T(8,128)} fusion(bf16[2,32,3,128,128]{4,3,2,1,0:T(8,128)(2,1)} %get-tuple-element.485, s32[]{:T(128)} %get-tuple-element.475, bf16[32,256,128]{2,1,0:T(8,128)(2,1)} %gather_fusion, pred[32]{0:T(512)(128)(4,1)S(1)} %get-tuple-element.443), kind=kOutput, calls=%fused_computation.45.clone.1 | convolution fusion | flops 537919488 | bytes 13632032 | tf_op jit(solution)/shard_map/while/body/eval_jaxpr/tsa,sgab->gtsb/dot_general | solution.py:60
  174.7 9.0 %copy.102 = f32[32,2,256,128]{3,2,1,0:T(8,128)} copy(f32[32,2,256,128]{2,3,1,0:T(8,128)} %convolution_bitcast_fusion.2) | data formatting | bytes 16777216 | tf_op jit(solution)/shard_map/while/body/eval_jaxpr/tsa,sgab->gtsb/transpose | solution.py:60
  183.7 18.6 %scatter_fusion = f32[2,256,26,128]{3,1,2,0:T(8,128)} fusion(f32[2,256,26,128]{3,1,2,0:T(8,128)} %get-tuple-element.476, s32[32]{0:T(128)S(1)} %fusion.68, f32[32,2,256,128]{3,2,1,0:T(8,128)} %copy.102), kind=kCustom, calls=%fused_computation.4.clone.1 | custom fusion | flops 2097152 | bytes 25165952 | tf_op jit(solution)/shard_map/while/body/eval_jaxpr/scatter-add | solution.py:63
  202.3 4.3 %gather_fusion = bf16[32,256,128]{2,1,0:T(8,128)(2,1)} fusion(bf16[256,64,128]{2,0,1:T(8,128)(2,1)} %get-tuple-element.487, s32[1024]{0:T(1024)S(1)} %pad_clamp_fusion.8), kind=kCustom, calls=%fused_computation.clone.clone.1 | custom fusion | bytes 4194432 | tf_op jit(solution)/shard_map/while/body/eval_jaxpr/jit(_take)/gather | solution.py:59
  206.7 6.8 %convolution_bitcast_fusion.2 = f32[32,2,256,128]{2,3,1,0:T(8,128)} fusion(bf16[2,32,3,128,128]{4,3,2,1,0:T(8,128)(2,1)} %get-tuple-element.485, s32[]{:T(128)} %get-tuple-element.475, bf16[32,256,128]{2,1,0:T(8,128)(2,1)} %gather_fusion, pred[32]{0:T(512)(128)(4,1)S(1)} %get-tuple-element.443), kind=kOutput, calls=%fused_computation.45.clone.1 | convolution fusion | flops 537919488 | bytes 13632032 | tf_op jit(solution)/shard_map/while/body/eval_jaxpr/tsa,sgab->gtsb/dot_general | solution.py:60
  213.5 9.0 %copy.102 = f32[32,2,256,128]{3,2,1,0:T(8,128)} copy(f32[32,2,256,128]{2,3,1,0:T(8,128)} %convolution_bitcast_fusion.2) | data formatting | bytes 16777216 | tf_op jit(solution)/shard_map/while/body/eval_jaxpr/tsa,sgab->gtsb/transpose | solution.py:60
  222.5 18.5 %scatter_fusion = f32[2,256,26,128]{3,1,2,0:T(8,128)} fusion(f32[2,256,26,128]{3,1,2,0:T(8,128)} %get-tuple-element.476, s32[32]{0:T(128)S(1)} %fusion.68, f32[32,2,256,128]{3,2,1,0:T(8,128)} %copy.102), kind=kCustom, calls=%fused_computation.4.clone.1 | custom fusion | flops 2097152 | bytes 25165952 | tf_op jit(solution)/shard_map/while/body/eval_jaxpr/scatter-add | solution.py:63
  240.9 4.9 %fusion.51 = (bf16[1,256,26,128]{3,1,2,0:T(8,128)(2,1)S(1)}, bf16[1,256,26,128]{3,1,2,0:T(8,128)(2,1)S(1)}, bf16[256,26,128]{2,0,1:T(8,128)(2,1)}) fusion(f32[2,256,26,128]{3,1,2,0:T(8,128)} %get-tuple-element.131, f32[256,26,128]{2,0,1:T(8,128)S(1)} %get-tuple-element.133), kind=kLoop, calls=%fused_computation.101 | loop fusion | flops 12779520 | bytes 15335424 | tf_op jit(solution)/shard_map/stack | solution.py:105
  246.2 4.3 %broadcast.152.clone.1 = f32[256,64,128]{2,0,1:T(8,128)} broadcast(f32[]{:T(128)} %constant.109.clone.1), dimensions={} | broadcast | bytes 8388612 | tf_op jit(solution)/shard_map/broadcast.20
  250.4 38.9 %while.43 = (s32[]{:T(128)}, f32[256,64,128]{2,0,1:T(8,128)}, s32[2,32]{1,0:T(2,128)S(1)}, bf16[2,32,3,128,128]{4,3,2,1,0:T(8,128)(2,1)}, s32[2,32]{1,0:T(2,128)...) while((s32[]{:T(128)}, f32[256,64,128]{2,0,1:T(8,128)}, s32[2,32]{1,0:T(2,128)S(1)}, ...), condition=%wide.region_12.14_spmd, body=%wide.region_10.13_spmd.sunk | while | flops 540018048 | bytes 54531732 | solution.py:24
  250.4 3.0 gather_fusion.3
  256.6 3.2 fusion.78
  259.9 10.0 %scatter_fusion.3 = f32[256,64,128]{2,0,1:T(8,128)} fusion(f32[256,64,128]{2,0,1:T(8,128)} %get-tuple-element.539, s32[32]{0:T(128)S(1)} %get-tuple-element.466, f32[32,256,128]{2,1,0:T(8,128)} %fusion.78), kind=kCustom, calls=%fused_computation.6.clone.1 | custom fusion | flops 1048576 | bytes 12583040 | tf_op jit(solution)/shard_map/while/body/eval_jaxpr/scatter-add | solution.py:113
  269.9 3.0 gather_fusion.3
  276.0 3.2 fusion.78
  279.3 10.0 %scatter_fusion.3 = f32[256,64,128]{2,0,1:T(8,128)} fusion(f32[256,64,128]{2,0,1:T(8,128)} %get-tuple-element.539, s32[32]{0:T(128)S(1)} %get-tuple-element.466, f32[32,256,128]{2,1,0:T(8,128)} %fusion.78), kind=kCustom, calls=%fused_computation.6.clone.1 | custom fusion | flops 1048576 | bytes 12583040 | tf_op jit(solution)/shard_map/while/body/eval_jaxpr/scatter-add | solution.py:113
  289.3 6.0 %copy_bitcast_fusion = bf16[256,8192]{1,0:T(8,128)(2,1)} fusion(f32[256,64,128]{2,0,1:T(8,128)} %get-tuple-element.134), kind=kLoop, calls=%fused_computation.81 | loop fusion | flops 2097152 | bytes 12582912 | tf_op jit(solution)/shard_map/convert_element_type | solution.py:119
  295.6 4.3 %broadcast.152.clone = f32[256,64,128]{2,0,1:T(8,128)} broadcast(f32[]{:T(128)} %constant.109.clone.1), dimensions={} | broadcast | bytes 8388612 | tf_op jit(solution)/shard_map/broadcast.20
  299.9 35.3 %while.41 = (s32[]{:T(128)}, f32[256,64,128]{2,0,1:T(8,128)}, s32[2,32]{1,0:T(2,128)S(1)}, bf16[2,32,3,128,128]{4,3,1,2,0:T(8,128)(2,1)}, s32[2,32]{1,0:T(2,128)S(1)}, /*index=5*/bf16[256,26,128]{2,0,1:T(8,128)(2,1)}, s32[]{:T(128)}) while((s32[]{:T(128)}, f32[256,64,128]{2,0,1:T(8,128)}, s32[2,32]{1,0:T(2,128)S(1)}, ...), condition=%wide.region_5.7_spmd, body=%wide.region_3.6_spmd.sunk | while | flops 270534016 | bytes 30414456 | solution.py:24
  304.6 2.7 fusion.71
  307.3 10.1 %scatter_fusion.1 = f32[256,64,128]{2,0,1:T(8,128)} fusion(f32[256,64,128]{2,0,1:T(8,128)} %get-tuple-element.518, s32[32]{0:T(128)S(1)} %get-tuple-element.450, f32[32,256,128]{2,1,0:T(8,128)} %fusion.71), kind=kCustom, calls=%fused_computation.5.clone.1 | custom fusion | flops 1048576 | bytes 12583040 | tf_op jit(solution)/shard_map/while/body/eval_jaxpr/scatter-add | solution.py:80
  322.3 2.7 fusion.71
  325.0 10.2 %scatter_fusion.1 = f32[256,64,128]{2,0,1:T(8,128)} fusion(f32[256,64,128]{2,0,1:T(8,128)} %get-tuple-element.518, s32[32]{0:T(128)S(1)} %get-tuple-element.450, f32[32,256,128]{2,1,0:T(8,128)} %fusion.71), kind=kCustom, calls=%fused_computation.5.clone.1 | custom fusion | flops 1048576 | bytes 12583040 | tf_op jit(solution)/shard_map/while/body/eval_jaxpr/scatter-add | solution.py:80
  335.2 6.0 %copy_bitcast_fusion.1 = bf16[256,8192]{1,0:T(8,128)(2,1)} fusion(f32[256,64,128]{2,0,1:T(8,128)} %get-tuple-element.132), kind=kLoop, calls=%fused_computation.82 | loop fusion | flops 2097152 | bytes 12582912 | tf_op jit(solution)/shard_map/convert_element_type | solution.py:86
  341.8 51.2 %reduce-scatter.3.cloned.1.call-done = bf16[256,1024]{1,0:T(8,128)(2,1)} async-done(((bf16[256,8192]{1,0:T(8,128)(2,1)}), bf16[256,1024]{1,0:T(8,128)(2,1)}) %reduce-scatter.3.cloned.1.call-update) | async-done | bytes 524304 | tf_op jit(solution)/shard_map/reduce_scatter | solution.py:85
  (76 shorter events, 23.4 us)
Async XLA Ops:
  7.2 41.0 %copy-start.4 = (s32[8]{0:T(128)S(1)}, s32[8]{0:T(128)}, u32[]{:S(2)}) copy-start(s32[8]{0:T(128)} %param.19) | copy-start | bytes 100
  7.2 47.3 %copy-start.3 = (s32[8,2]{0,1:T(2,128)S(1)}, s32[8,2]{0,1:T(2,128)}, u32[]{:S(2)}) copy-start(s32[8,2]{0,1:T(2,128)} %param.18) | copy-start | bytes 196
  7.2 112.2 %all-gather.4.cloned.1.call-start = ((), (), s32[]{:S(2)}) async-start(), calls=%async_computation.5 | async-start | bytes 7864320 | tf_op jit(solution)/shard_map/all_gather | solution.py:42
  48.8 33.4 %all-to-all-start.1 = ((s32[8,1,1]{2,1,0:T(1,128)}), s32[8,1,1]{2,1,0:T(1,128)S(1)}, u32[]{:S(2)}, u32[]{:S(2)}) async-start(s32[8,1,1]{2,1,0:T(1,128)} %copy.83), calls=%async_computation.1 | async-start | bytes 8192 | tf_op jit(solution)/shard_map/all_to_all | solution.py:39
  74.6 6.4 %copy-start.5 = (u32[32]{0:T(128)S(1)}, u32[32]{0:T(128)}, u32[]{:S(2)}) copy-start(u32[32]{0:T(128)} %constant.120) | copy-start | bytes 388
  82.3 13.4 %all-to-all-start = ((s32[8,1,2]{2,1,0:T(1,128)}), s32[8,1,2]{2,1,0:T(1,128)S(1)}, u32[]{:S(2)}, u32[]{:S(2)}) async-start(s32[8,1,2]{2,1,0:T(1,128)} %copy.78), calls=%async_computation | async-start | bytes 8192 | tf_op jit(solution)/shard_map/all_to_all | solution.py:38
  87.4 254.4 %reduce-scatter.5.cloned.1.call-start = ((), (), s32[]{:S(2)}) async-start(), calls=%async_computation.7 | async-start | bytes 4718592 | tf_op jit(solution)/shard_map/reduce_scatter | solution.py:118
  122.6 4.5 %copy-start = (bf16[2,32,3,128,128]{4,3,2,1,0:T(8,128)(2,1)}, bf16[2,32,3,128,128]{4,3,2,1,0:T(8,128)(2,1)S(1)}, u32[]{:S(2)}) copy-start(bf16[2,32,3,128,128]{4,3,2,1,0:T(8,128)(2,1)S(1)} %bitcast_select_fusion) | copy-start | bytes 18874372
  132.1 2.5 copy-start.1
  148.2 2.5 copy-start.1
  253.5 3.1 copy-start.2
  272.9 3.1 copy-start.2
  295.3 97.6 %reduce-scatter.3.cloned.1.call-start = ((), (), s32[]{:S(2)}) async-start(), calls=%async_computation.6 | async-start | bytes 4718592 | tf_op jit(solution)/shard_map/reduce_scatter | solution.py:85
Sparse Core Ops, SparseCore 0:
  48.3 71.0 all-gather.3
  295.5 46.3 reduce-scatter.4
  344.7 48.2 reduce-scatter.2
where the time goes:
time: 406 us; the launch traced here: 400 us
  other arithmetic  111 us (27%)
  local copies, waits for them, and re-layouts  108 us (27%)
  waiting for transfers between devices  67.7 us (17%)
  blocking collectives  55.7 us (14%)
  matrix products  30.9 us (8%)
  between operations  14.5 us (4%)
  starting transfers between devices  11.1 us (3%)
    reduce_scatter x1, waiting for transfers between devices, body(): lax.psum_scatter(out_part.astype(jnp.bfloat16), 'tensor', scatter_dimensi...  51.2 us
    all_to_all x1, blocking collectives, body(): lax.all_to_all(weight_tiles, 'tensor', split_axis=0, concat_axis=0, tiled...  40.9 us
    scatter-add x2, other arithmetic, gate_up_step(): return acc_value.at[:, :, col_block, :].add(products)  37.1 us
    scatter-add x2, other arithmetic, down_step(): return acc_value.at[:, row_block, :].add(products)  20.3 us
    scatter-add x2, other arithmetic, input_step(): return acc_value.at[:, row_block, :].add(products)  20 us
    transpose x2, local copies, waits for them, and re-layouts, gate_up_step(): jnp.einsum('tsa,sgab->gtsb', gathered, weights[:, 0:2], preferred_element...  17.9 us
    while x3, local copies, waits for them, and re-layouts, over_blocks(): running, _ = lax.scan(advance, running, shaped)  17.3 us
    all_gather x1, waiting for transfers between devices, body(): lax.all_gather(arrived_tiles, 'dp', axis=0, tiled=True)  15.9 us
  transfers between devices with their start and end apart: 5, of which 3 were waited for; matrix products, arithmetic and copies ran while one was open for 19% of the time, Pallas kernels for 0%

commit v1 on v0

v1 whole, which is shorter than its diff:
```python
import functools

import jax
import jax.numpy as jnp
from jax import lax
from jax.experimental import pallas as pl
from jax.experimental.pallas import tpu as pltpu
from jax.sharding import PartitionSpec as P

FF = 26624
GROUP = 8
F32 = jnp.float32
NT = (((1,), (1,)), ((), ()))


def local_kernel(dims, row_ref, col_ref, row_to_ref, col_to_ref, tok_ref, grad_ref, tile_ref, out_ref,
                 pre, back, hid, pair, acc_out, acc_in):
    rows, cols, owners, side, group = dims
    phase, block = pl.program_id(0), pl.program_id(1)
    blocks = pl.num_programs(1)
    per = rows // owners

    @pl.when((phase == 0) & (block == 0))
    def _():
        @pl.loop(0, cols)
        def _(i):
            pre[i] = jnp.zeros(pre.shape[1:], F32)
            back[i] = jnp.zeros(back.shape[1:], F32)

    @pl.when(phase == 0)
    def _():
        for j in range(group):
            s = block * group + j
            at = pl.ds(pl.multiple_of(row_ref[s] * side, side), side)
            to = col_to_ref[s]
            both = jnp.concatenate([tile_ref[j, 0], tile_ref[j, 1]], axis=1)
            pre[to] += jnp.dot(tok_ref[:, at], both, preferred_element_type=F32)
            back[to] += lax.dot_general(grad_ref[:, at], tile_ref[j, 2], NT, preferred_element_type=F32)

    @pl.when((phase == 1) & (block == 0))
    def _():
        @pl.loop(0, cols)
        def _(i):
            gate = pre[i, :, :side]
            up = pre[i, :, side:]
            gh = back[i]
            s = jax.nn.sigmoid(gate)
            act = gate * s
            hid[i] = (act * up).astype(jnp.bfloat16)
            pair[i, :, :side] = (gh * up * (s * (1.0 + gate * (1.0 - s)))).astype(jnp.bfloat16)
            pair[i, :, side:] = (gh * act).astype(jnp.bfloat16)

        @pl.loop(0, rows)
        def _(i):
            acc_out[i] = jnp.zeros(acc_out.shape[1:], F32)
            acc_in[i] = jnp.zeros(acc_in.shape[1:], F32)

    @pl.when(phase == 1)
    def _():
        for j in range(group):
            s = block * group + j
            c = col_ref[s]
            to = row_to_ref[s]
            both = jnp.concatenate([tile_ref[j, 0], tile_ref[j, 1]], axis=1)
            acc_out[to] += jnp.dot(hid[c], tile_ref[j, 2], preferred_element_type=F32)
            acc_in[to] += lax.dot_general(pair[c], both, NT, preferred_element_type=F32)

    @pl.when((phase == 1) & (block == blocks - 1))
    def _():
        @pl.loop(0, owners)
        def _(k):
            for i in range(per):
                out_ref[k, 0, i] = acc_out[k * per + i].astype(jnp.bfloat16)
                out_ref[k, 1, i] = acc_in[k * per + i].astype(jnp.bfloat16)


def local_pass(tokens, out_grad, tiles, row, col, row_to, col_to, owners, cols):
    toks, feats = tokens.shape
    slots, _, side, _ = tiles.shape
    rows = feats // side
    whole = lambda p, b, *_: (0, 0)
    once = pl.Buffered(1)
    return pl.pallas_call(
        functools.partial(local_kernel, (rows, cols, owners, side, GROUP)),
        out_shape=jax.ShapeDtypeStruct((owners, 2, rows // owners, toks, side), jnp.bfloat16),
        grid_spec=pltpu.PrefetchScalarGridSpec(
            num_scalar_prefetch=4,
            grid=(2, slots // GROUP),
            in_specs=[
                pl.BlockSpec((toks, feats), whole, pipeline_mode=once),
                pl.BlockSpec((toks, feats), whole, pipeline_mode=once),
                pl.BlockSpec((GROUP, 3, side, side), lambda p, b, *_: (b, 0, 0, 0)),
            ],
            out_specs=pl.BlockSpec((owners, 2, rows // owners, toks, side), lambda p, b, *_: (0, 0, 0, 0, 0), pipeline_mode=once),
            scratch_shapes=[
                pltpu.VMEM((cols + 1, toks, 2 * side), F32),
                pltpu.VMEM((cols + 1, toks, side), F32),
                pltpu.VMEM((cols, toks, side), jnp.bfloat16),
                pltpu.VMEM((cols, toks, 2 * side), jnp.bfloat16),
                pltpu.VMEM((rows + 1, toks, side), F32),
                pltpu.VMEM((rows + 1, toks, side), F32),
            ],
        ),
        compiler_params=pltpu.CompilerParams(vmem_limit_bytes=58 * 2**20),
        cost_estimate=pl.CostEstimate(flops=12 * slots * toks * side * side, bytes_accessed=30 * 2**20, transcendentals=0),
    )(row, col, row_to, col_to, tokens, out_grad, tiles)


def body(tokens, out_grad, weight_tiles, tile_places, live_counts):
    toks, feats = tokens.shape
    side = weight_tiles.shape[-1]
    peer = weight_tiles.shape[1]
    rows = feats // side
    owners = lax.axis_size("tensor")
    cols = FF // (side * owners)
    meta = jnp.concatenate([tile_places, live_counts[:, None]], axis=1)
    meta = lax.all_gather(meta, ("dp", "tensor"), axis=0)
    mine = lax.dynamic_index_in_dim(meta, lax.axis_index("tensor"), axis=1, keepdims=False)
    places = mine[:, :peer]
    live = (jnp.arange(peer)[None, :] < mine[:, peer:]).reshape(-1)
    row = (places // cols).reshape(-1)
    col = (places % cols).reshape(-1)
    row_to = jnp.where(live, row, rows)
    col_to = jnp.where(live, col, cols)
    tiles = lax.all_to_all(weight_tiles, "tensor", split_axis=0, concat_axis=0, tiled=True)
    tiles = lax.all_gather(tiles, "dp", axis=0, tiled=True)
    tiles = tiles.reshape((-1,) + tiles.shape[2:])
    parts = local_pass(tokens, out_grad, tiles, row, col, row_to, col_to, owners, cols)
    total = lax.psum_scatter(parts, "tensor", scatter_dimension=0, tiled=True)
    total = jnp.transpose(total[0], (0, 2, 1, 3)).reshape(2, toks, feats // owners)
    return total[0], total[1]


def solution(mesh):
    in_specs = (
        P("dp", None),
        P("dp", None),
        P(("dp", "tensor"), None, None, None, None),
        P(("dp", "tensor"), None),
        P(("dp", "tensor")),
    )
    out_specs = (P("dp", "tensor"), P("dp", "tensor"))
    return jax.shard_map(body, mesh=mesh, in_specs=in_specs, out_specs=out_specs, check_vma=False)
```

time: 406 us -> 248 us (0.61)
  other arithmetic: 111 us -> 0.68 us
  local copies, waits for them, and re-layouts: 108 us -> 4.43 us
  waiting for transfers between devices: 67.7 us -> 121 us
  matrix products: 30.9 us -> 0 us
  Pallas kernels: 0 us -> 26 us
  blocking collectives: 55.7 us -> 76.6 us
  starting transfers between devices: 11.1 us -> 0.08 us
    scatter-add x8 -> x0, other arithmetic: 90.4 us -> none  [the longest x2 37.1 us: gate_up_step(): return acc_value.at[:, :, col_block, :].add(products)]
    reduce_scatter x2 -> x1, waiting for transfers between devices: 51.8 us -> 87 us  [body(): total = lax.psum_scatter(parts, 'tensor', scatter_dimension=0, tiled=True)]
    dot_general x8 -> x0, matrix products: 30.9 us -> none  [the longest x2 13.6 us: gate_up_step(): jnp.einsum('tsa,sgab->gtsb', gathered, weights[:, 0:2], preferred_element...]
    all_gather x1, blocking collectives: 7.38 us -> 35.7 us  [body(): meta = lax.all_gather(meta, ('dp', 'tensor'), axis=0)]
    gather x8 -> x0, local copies, waits for them, and re-layouts: 28.3 us -> none  [the longest x2 8.69 us: back_step(): gathered = jnp.take(grad_blocks, row_block, axis=1)]
    pallas_call x0 -> x1, Pallas kernels: none -> 26 us  [local_pass(): pl.pallas_call(functools.partial(local_kernel, (rows, cols, owners, side,...]
    while x11 -> x0, local copies, waits for them, and re-layouts: 19.2 us -> none  [the longest x3 17.3 us: over_blocks(): running, _ = lax.scan(advance, running, shaped)]
    all_gather x1, waiting for transfers between devices: 15.9 us -> 34 us  [body(): tiles = lax.all_gather(tiles, 'dp', axis=0, tiled=True)]
  transfers between devices with their start and end apart: 5 -> 2, of which waited for: 3 -> 2; matrix products, arithmetic and copies ran while one was open for 19% -> 1% of each run, Pallas kernels for 0% -> 0%
where the time goes in v1:
time: 248 us; the launch traced here: 243 us
  waiting for transfers between devices  121 us (49%)
  blocking collectives  76.6 us (31%)
  Pallas kernels  26 us (10%)
  between operations  14.1 us (6%)
  local copies, waits for them, and re-layouts  4.43 us (2%)
    reduce_scatter x1, waiting for transfers between devices, body(): total = lax.psum_scatter(parts, 'tensor', scatter_dimension=0, tiled=True)  87 us
    all_to_all x1, blocking collectives, body(): lax.all_to_all(weight_tiles, 'tensor', split_axis=0, concat_axis=0, tiled...  40.9 us
    all_gather x1, blocking collectives, body(): meta = lax.all_gather(meta, ('dp', 'tensor'), axis=0)  35.7 us
    all_gather x1, waiting for transfers between devices, body(): tiles = lax.all_gather(tiles, 'dp', axis=0, tiled=True)  34 us
    pallas_call x1, Pallas kernels, local_pass(): pl.pallas_call(functools.partial(local_kernel, (rows, cols, owners, side,...  26 us
  transfers between devices with their start and end apart: 2, of which 2 were waited for; matrix products, arithmetic and copies ran while one was open for 1% of the time, Pallas kernels for 0%

profile of v1, /device:TPU:10, one launch (start us, length us, event | category | flops | bytes accessed | tf_op | source)
XLA Modules:
  0.0 242.9 jit_solution(4691024794266888554)
XLA Ops:
  7.2 0.0 copy-start.3
  7.2 0.0 copy-start.2
  7.2 0.0 all-gather.4.cloned.1.call-start
  7.2 40.9 %all_to_all.5 = bf16[8,2,3,128,128]{4,3,2,1,0:T(8,128)(2,1)} all-to-all(bf16[8,2,3,128,128]{4,3,2,1,0:T(8,128)(2,1)} %param.7), channel_id=1, replica_groups=mesh['dp'=4,'tensor'=8] {'tensor'}, dimensions={0} | all-to-all | bytes 3145728 | tf_op jit(solution)/shard_map/all_to_all | solution.py:125
  48.1 0.0 all-gather.4.cloned.1.call-update
  48.1 0.0 reduce-scatter.2.cloned.1.call-start
  48.2 0.0 copy-done.3
  48.2 0.0 copy-done.2
  48.2 35.7 %all-gather.1 = s32[32,8,3]{1,2,0:T(4,128)S(1)} all-gather(s32[1,8,3]{1,2,0:T(4,128)S(1)} %add_bitcast_fusion), channel_id=2, replica_groups=mesh['dp'=4,'tensor'=8] {'dp','tensor'}, dimensions={0}, use_global_device_ids=true | all-gather | bytes 3168 | tf_op jit(solution)/shard_map/all_gather | solution.py:117
  84.0 0.1 constant_dynamic-slice_fusion
  84.1 0.1 copy.17
  84.2 0.1 iota_compare_fusion
  84.2 0.1 lt.35
  84.4 0.1 copy.19
  84.5 0.1 reshape.23.col_ref
  84.6 0.0 copy-start
  84.6 0.1 copy.18
  84.7 0.1 reshape.22.row_ref
  84.8 0.0 copy-start.1
  84.8 0.6 broadcast_select_fusion
  85.4 34.0 %all-gather.4.cloned.1.call-done = bf16[32,2,3,128,128]{4,3,2,1,0:T(8,128)(2,1)} async-done(((bf16[8,2,3,128,128]{4,3,2,1,0:T(8,128)(2,1)}), bf16[32,2,3,128,128]{4,3,2,1,0:T(8,128)(2,1)}) %all-gather.4.cloned.1.call-update) | async-done | bytes 6291472 | tf_op jit(solution)/shard_map/all_gather | solution.py:126
  119.4 0.0 copy-done
  119.4 0.0 copy-done.1
  119.4 26.0 %shard_map.68 = bf16[8,2,8,256,128]{4,3,2,1,0:T(8,128)(2,1)} custom-call(s32[64]{0:T(128)} %copy-done.1, s32[64]{0:T(128)} %copy-done, s32[64]{0:T(128)} %get-tuple-element.11.row_to_ref, s32[64]{0:T(128)} %get-tuple-element.10.col_to_ref, bf16[256,8192]{1,0:T(8,128)(2,1)} %tok_ref.1, bf16[256,8192]{1,0:T(8,128)(2,1)} %grad_ref.1, ...), custom_call_target="tpu_custom_call" | custom-call | flops 3221225472 | bytes 31457280 | tf_op jit(solution)/shard_map/pallas_call | solution.py:83
  145.4 0.0 reduce-scatter.2.cloned.1.call-update
  145.4 87.0 %reduce-scatter.2.cloned.1.call-done = bf16[1,2,8,256,128]{4,3,2,1,0:T(8,128)(2,1)} async-done(((bf16[8,2,8,256,128]{4,3,2,1,0:T(8,128)(2,1)}), bf16[1,2,8,256,128]{4,3,2,1,0:T(8,128)(2,1)}) %reduce-scatter.2.cloned.1.call-update) | async-done | bytes 1048592 | tf_op jit(solution)/shard_map/reduce_scatter | solution.py:129
  232.4 1.3 fusion
  233.7 0.2 copy.21
  233.9 1.0 copy.23
  234.9 0.2 copy.20
  235.1 1.0 copy.22
  (3 shorter events, 0.0 us)
Async XLA Ops:
  7.2 41.0 %copy-start.3 = (s32[8]{0:T(128)S(1)}, s32[8]{0:T(128)}, u32[]{:S(2)}) copy-start(s32[8]{0:T(128)} %param.9) | copy-start | bytes 100
  7.2 41.0 %copy-start.2 = (s32[8,2]{0,1:T(2,128)S(1)}, s32[8,2]{0,1:T(2,128)}, u32[]{:S(2)}) copy-start(s32[8,2]{0,1:T(2,128)} %param.8) | copy-start | bytes 196
  7.2 112.2 %all-gather.4.cloned.1.call-start = ((), (), s32[]{:S(2)}) async-start(), calls=%async_computation.2 | async-start | bytes 7864320 | tf_op jit(solution)/shard_map/all_gather | solution.py:126
  48.1 184.3 %reduce-scatter.2.cloned.1.call-start = ((), (), s32[]{:S(2)}) async-start(), calls=%async_computation.3 | async-start | bytes 9437184 | tf_op jit(solution)/shard_map/reduce_scatter | solution.py:129
  84.6 34.8 %copy-start = (s32[64]{0:T(128)}, s32[64]{0:T(128)S(1)}, u32[]{:S(2)}) copy-start(s32[64]{0:T(128)S(1)} %reshape.23.col_ref) | copy-start | bytes 772
  84.8 34.6 %copy-start.1 = (s32[64]{0:T(128)}, s32[64]{0:T(128)S(1)}, u32[]{:S(2)}) copy-start(s32[64]{0:T(128)S(1)} %reshape.22.row_ref) | copy-start | bytes 772
Sparse Core Ops, SparseCore 0:
  48.3 71.0 all-gather.3
  145.5 86.7 reduce-scatter.1

commit v2 on v1

--- a/solution.py
+++ b/solution.py
@@ -11,11 +11,87 @@
 GROUP = 8
 F32 = jnp.float32
 NT = (((1,), (1,)), ((), ()))
+MESH = pl.DeviceIdType.MESH
+META = 16
+
+
+def near_first(n):
+    order = []
+    for o in range(1, n // 2 + 1):
+        order += [o] if 2 * o == n else [o, n - o]
+    return order
+
+
+def spread_kernel(n_dp, owners, block_ref, out_ref, own_sem, send_a, recv_a, send_b, recv_b):
+    d, t = lax.axis_index("dp"), lax.axis_index("tensor")
+    barrier = pltpu.get_barrier_semaphore()
+    for o in range(1, owners):
+        pl.semaphore_signal(barrier, inc=1, device_id=(d, lax.rem(t + o, owners)), device_id_type=MESH)
+    for e in range(1, n_dp):
+        pl.semaphore_signal(barrier, inc=1, device_id=(lax.rem(d + e, n_dp), t), device_id_type=MESH)
+    pl.semaphore_wait(barrier, owners - 1 + n_dp - 1)
+
+    own = pltpu.make_async_copy(block_ref.at[t], out_ref.at[d, t], own_sem)
+    own.start()
+    first, second = {}, []
+
+    def forward(src, slot, o):
+        for e in range(1, n_dp):
+            copy = pltpu.make_async_remote_copy(
+                src_ref=src, dst_ref=out_ref.at[d, slot],
+                send_sem=send_b.at[e - 1, o], recv_sem=recv_b.at[e - 1, o],
+                device_id=(lax.rem(d + e, n_dp), t), device_id_type=MESH)
+            copy.start()
+            second.append(copy)
+
+    order = near_first(owners)
+    for o in order:
+        to = lax.rem(t + o, owners)
+        first[o] = pltpu.make_async_remote_copy(
+            src_ref=block_ref.at[to], dst_ref=out_ref.at[d, t],
+            send_sem=send_a.at[o - 1], recv_sem=recv_a.at[o - 1],
+            device_id=(d, to), device_id_type=MESH)
+        first[o].start()
+    forward(block_ref.at[t], t, 0)
+    for o in order:
+        first[o].wait_recv()
+        slot = lax.rem(t + owners - o, owners)
+        forward(out_ref.at[d, slot], slot, o)
+    own.wait()
+    for o in order:
+        first[o].wait_send()
+    for copy in second:
+        copy.wait()
+
+
+def spread(blocks, n_dp):
+    owners, length, side = blocks.shape
+    return pl.pallas_call(
+        functools.partial(spread_kernel, n_dp, owners),
+        out_shape=jax.ShapeDtypeStruct((n_dp, owners, length, side), blocks.dtype),
+        in_specs=[pl.BlockSpec(memory_space=pl.ANY)],
+        out_specs=pl.BlockSpec(memory_space=pl.ANY),
+        scratch_shapes=[
+            pltpu.SemaphoreType.DMA(()),
+            pltpu.SemaphoreType.DMA((owners - 1,)),
+            pltpu.SemaphoreType.DMA((owners - 1,)),
+            pltpu.SemaphoreType.DMA((n_dp - 1, owners)),
+            pltpu.SemaphoreType.DMA((n_dp - 1, owners)),
+        ],
+        compiler_params=pltpu.CompilerParams(collective_id=0, has_side_effects=True),
+        cost_estimate=pl.CostEstimate(flops=0, bytes_accessed=2 * n_dp * blocks.size * 2, transcendentals=0),
+    )(blocks)
+
+
+def tile_of(tile_ref, peer, j, g):
+    side = tile_ref.shape[-1]
+    at = (j % peer * 3 + g) * side
+    return tile_ref[j // peer, at:at + side]
 
 
 def local_kernel(dims, row_ref, col_ref, row_to_ref, col_to_ref, tok_ref, grad_ref, tile_ref, out_ref,
                  pre, back, hid, pair, acc_out, acc_in):
-    rows, cols, owners, side, group = dims
+    rows, cols, owners, side, peer, group = dims
     phase, block = pl.program_id(0), pl.program_id(1)
     blocks = pl.num_programs(1)
     per = rows // owners
@@ -33,9 +109,9 @@
             s = block * group + j
             at = pl.ds(pl.multiple_of(row_ref[s] * side, side), side)
             to = col_to_ref[s]
-            both = jnp.concatenate([tile_ref[j, 0], tile_ref[j, 1]], axis=1)
+            both = jnp.concatenate([tile_of(tile_ref, peer, j, 0), tile_of(tile_ref, peer, j, 1)], axis=1)
             pre[to] += jnp.dot(tok_ref[:, at], both, preferred_element_type=F32)
-            back[to] += lax.dot_general(grad_ref[:, at], tile_ref[j, 2], NT, preferred_element_type=F32)
+            back[to] += lax.dot_general(grad_ref[:, at], tile_of(tile_ref, peer, j, 2), NT, preferred_element_type=F32)
 
     @pl.when((phase == 1) & (block == 0))
     def _():
@@ -61,8 +137,8 @@
             s = block * group + j
             c = col_ref[s]
             to = row_to_ref[s]
-            both = jnp.concatenate([tile_ref[j, 0], tile_ref[j, 1]], axis=1)
-            acc_out[to] += jnp.dot(hid[c], tile_ref[j, 2], preferred_element_type=F32)
+            both = jnp.concatenate([tile_of(tile_ref, peer, j, 0), tile_of(tile_ref, peer, j, 1)], axis=1)
+            acc_out[to] += jnp.dot(hid[c], tile_of(tile_ref, peer, j, 2), preferred_element_type=F32)
             acc_in[to] += lax.dot_general(pair[c], both, NT, preferred_element_type=F32)
 
     @pl.when((phase == 1) & (block == blocks - 1))
@@ -74,14 +150,15 @@
                 out_ref[k, 1, i] = acc_in[k * per + i].astype(jnp.bfloat16)
 
 
-def local_pass(tokens, out_grad, tiles, row, col, row_to, col_to, owners, cols):
+def local_pass(tokens, out_grad, tiles, row, col, row_to, col_to, owners, cols, peer):
     toks, feats = tokens.shape
-    slots, _, side, _ = tiles.shape
+    sources, length, side = tiles.shape
+    slots = sources * peer
     rows = feats // side
     whole = lambda p, b, *_: (0, 0)
     once = pl.Buffered(1)
     return pl.pallas_call(
-        functools.partial(local_kernel, (rows, cols, owners, side, GROUP)),
+        functools.partial(local_kernel, (rows, cols, owners, side, peer, GROUP)),
         out_shape=jax.ShapeDtypeStruct((owners, 2, rows // owners, toks, side), jnp.bfloat16),
         grid_spec=pltpu.PrefetchScalarGridSpec(
             num_scalar_prefetch=4,
@@ -89,7 +166,7 @@
             in_specs=[
                 pl.BlockSpec((toks, feats), whole, pipeline_mode=once),
                 pl.BlockSpec((toks, feats), whole, pipeline_mode=once),
-                pl.BlockSpec((GROUP, 3, side, side), lambda p, b, *_: (b, 0, 0, 0)),
+                pl.BlockSpec((GROUP // peer, length, side), lambda p, b, *_: (b, 0, 0)),
             ],
             out_specs=pl.BlockSpec((owners, 2, rows // owners, toks, side), lambda p, b, *_: (0, 0, 0, 0, 0), pipeline_mode=once),
             scratch_shapes=[
@@ -113,19 +190,21 @@
     rows = feats // side
     owners = lax.axis_size("tensor")
     cols = FF // (side * owners)
-    meta = jnp.concatenate([tile_places, live_counts[:, None]], axis=1)
-    meta = lax.all_gather(meta, ("dp", "tensor"), axis=0)
-    mine = lax.dynamic_index_in_dim(meta, lax.axis_index("tensor"), axis=1, keepdims=False)
-    places = mine[:, :peer]
-    live = (jnp.arange(peer)[None, :] < mine[:, peer:]).reshape(-1)
-    row = (places // cols).reshape(-1)
-    col = (places % cols).reshape(-1)
+    n_dp = lax.axis_size("dp")
+    live = jnp.arange(peer)[None, :] < live_counts[:, None]
+    meta = jnp.concatenate([tile_places // cols, tile_places % cols, live.astype(jnp.int32)], axis=1)
+    meta = jnp.pad(meta.astype(jnp.bfloat16), ((0, 0), (0, side - 3 * peer)))
+    meta = jnp.broadcast_to(meta[:, None, :], (owners, META, side))
+    blocks = jnp.concatenate([weight_tiles.reshape(owners, -1, side), meta], axis=1)
+    tiles = spread(blocks, n_dp)
+    tiles = tiles.reshape((n_dp * owners,) + tiles.shape[2:])
+    meta = tiles[:, -META, :3 * peer].astype(jnp.int32)
+    row = meta[:, :peer].reshape(-1)
+    col = meta[:, peer:2 * peer].reshape(-1)
+    live = meta[:, 2 * peer:].reshape(-1) > 0
     row_to = jnp.where(live, row, rows)
     col_to = jnp.where(live, col, cols)
-    tiles = lax.all_to_all(weight_tiles, "tensor", split_axis=0, concat_axis=0, tiled=True)
-    tiles = lax.all_gather(tiles, "dp", axis=0, tiled=True)
-    tiles = tiles.reshape((-1,) + tiles.shape[2:])
-    parts = local_pass(tokens, out_grad, tiles, row, col, row_to, col_to, owners, cols)
+    parts = local_pass(tokens, out_grad, tiles, row, col, row_to, col_to, owners, cols, peer)
     total = lax.psum_scatter(parts, "tensor", scatter_dimension=0, tiled=True)
     total = jnp.transpose(total[0], (0, 2, 1, 3)).reshape(2, toks, feats // owners)
     return total[0], total[1]

time: 248 us -> 216 us (0.87)
  the two profiles are of different devices: /device:TPU:10 before, /device:TPU:0 now
where the time goes in v2:
time: 216 us
  Pallas kernels  104 us (48%)
  waiting for transfers between devices  88.2 us (41%)
  between operations  14.1 us (7%)
  other arithmetic  5.57 us (3%)
  local copies, waits for them, and re-layouts  4.22 us (2%)
    reduce_scatter x1, waiting for transfers between devices, body(): total = lax.psum_scatter(parts, 'tensor', scatter_dimension=0, tiled=True)  88.2 us
    pallas_call x1, Pallas kernels, spread(): pl.pallas_call(functools.partial(spread_kernel, n_dp, owners), out_shape=...  77.6 us
    pallas_call x1, Pallas kernels, local_pass(): pl.pallas_call(functools.partial(local_kernel, (rows, cols, owners, side,...  26 us
  transfers between devices with their start and end apart: 1, of which 1 were waited for; matrix products, arithmetic and copies ran while one was open for 0% of the time, Pallas kernels for 0%

profile of v2, /device:TPU:0, one launch (start us, length us, event | category | flops | bytes accessed | tf_op | source)
XLA Modules:
  0.0 215.8 jit_solution(8890966301474865795)
XLA Ops:
  7.2 0.0 reduce-scatter.2.cloned.1.call-start
  7.2 0.7 fusion
  7.9 0.7 fusion.2
  8.6 0.1 copy.13
  8.7 2.7 %pad_maximum_fusion.block_ref = bf16[8,784,128]{2,1,0:T(8,128)(2,1)} fusion(bf16[8,16,128]{2,1,0:T(8,128)(2,1)S(1)} %broadcast_in_dim.15, bf16[8,768,128]{2,1,0:T(8,128)(2,1)} %bitcast.12), kind=kLoop, calls=%fused_computation | loop fusion | flops 3211264 | bytes 3211264 | tf_op jit(solution)/shard_map/concatenate | solution.py:198
  11.4 77.6 %shard_map.68 = bf16[4,8,784,128]{3,2,1,0:T(8,128)(2,1)} custom-call(bf16[8,784,128]{2,1,0:T(8,128)(2,1)} %pad_maximum_fusion.block_ref), custom_call_target="tpu_custom_call" | custom-call | bytes 12845056 | tf_op jit(solution)/shard_map/pallas_call | solution.py:69
  89.0 0.9 slice_convert_fusion
  89.8 0.1 slice_compare_fusion
  89.9 0.1 fusion.4
  90.0 0.1 gt.11
  90.1 0.1 reshape.31.col_ref
  90.2 0.0 copy-start
  90.2 0.1 reshape.30.row_ref
  90.3 0.0 copy-start.1
  90.3 0.6 broadcast_select_fusion
  90.9 0.0 copy-done
  90.9 0.0 copy-done.1
  90.9 26.0 %shard_map.69 = bf16[8,2,8,256,128]{4,3,2,1,0:T(8,128)(2,1)} custom-call(s32[64]{0:T(128)} %copy-done.1, s32[64]{0:T(128)} %copy-done, s32[64]{0:T(128)} %get-tuple-element.11.row_to_ref, s32[64]{0:T(128)} %get-tuple-element.10.col_to_ref, bf16[256,8192]{1,0:T(8,128)(2,1)} %tok_ref.1, bf16[256,8192]{1,0:T(8,128)(2,1)} %grad_ref.1, bf16[32,784,128]{2,1,0:T(8,128)(2,1)} %bitcast.9), custom_call_target="tpu_custom_call" | custom-call | flops 3221225472 | bytes 31457280 | tf_op jit(solution)/shard_map/pallas_call | solution.py:160
  117.0 0.0 reduce-scatter.2.cloned.1.call-update
  117.0 88.2 %reduce-scatter.2.cloned.1.call-done = bf16[1,2,8,256,128]{4,3,2,1,0:T(8,128)(2,1)} async-done(((bf16[8,2,8,256,128]{4,3,2,1,0:T(8,128)(2,1)}), bf16[1,2,8,256,128]{4,3,2,1,0:T(8,128)(2,1)}) %reduce-scatter.2.cloned.1.call-update) | async-done | bytes 1048592 | tf_op jit(solution)/shard_map/reduce_scatter | solution.py:208
  205.2 1.3 fusion.3
  206.5 0.2 copy.10
  206.7 1.0 copy.12
  207.7 0.2 copy.9
  207.9 1.0 copy.11
  (3 shorter events, 0.0 us)
Async XLA Ops:
  7.2 198.1 %reduce-scatter.2.cloned.1.call-start = ((), (), s32[]{:S(2)}) async-start(), calls=%async_computation.1 | async-start | bytes 9437184 | tf_op jit(solution)/shard_map/reduce_scatter | solution.py:208
  90.2 0.7 copy-start
  90.3 0.6 copy-start.1
Sparse Core Ops, SparseCore 0:
  117.1 88.0 reduce-scatter.1

commit v3 on v2

--- a/solution.py
+++ b/solution.py
@@ -64,10 +64,71 @@
         copy.wait()
 
 
+def square_kernel(n_dp, owners, block_ref, out_ref, own_sem, send_a, recv_a, send_b, recv_b):
+    d, t = lax.axis_index("dp"), lax.axis_index("tensor")
+    beside = (d + 1 - 2 * lax.rem(d, 2), lax.rem(d + 2, 4))
+    barrier = pltpu.get_barrier_semaphore()
+    for o in range(1, owners):
+        pl.semaphore_signal(barrier, inc=1, device_id=(d, lax.rem(t + o, owners)), device_id_type=MESH)
+    for to in beside:
+        pl.semaphore_signal(barrier, inc=1, device_id=(to, t), device_id_type=MESH)
+    pl.semaphore_wait(barrier, owners - 1 + 2)
+
+    def send(src, row, slot, to, kind, o):
+        copy = pltpu.make_async_remote_copy(
+            src_ref=src, dst_ref=out_ref.at[row, slot],
+            send_sem=send_b.at[kind, o], recv_sem=recv_b.at[kind, o],
+            device_id=(to, t), device_id_type=MESH)
+        copy.start()
+        return copy
+
+    order = near_first(owners)
+    first, direct, passed = {}, {}, []
+
+    def outward(src, o):
+        slot = lax.rem(t + owners - o, owners)
+        direct[o] = [send(src, d, slot, beside[kind], kind, o) for kind in range(2)]
+
+    def onward(i, o):
+        slot = lax.rem(t + owners - o, owners)
+        via = i % 2
+        direct[o][via].wait_recv()
+        passed.append(send(out_ref.at[beside[via], slot], beside[via], slot, beside[1 - via], 2, o))
+
+    outward(block_ref.at[t], 0)
+    for o in order:
+        to = lax.rem(t + o, owners)
+        first[o] = pltpu.make_async_remote_copy(
+            src_ref=block_ref.at[to], dst_ref=out_ref.at[d, t],
+            send_sem=send_a.at[o - 1], recv_sem=recv_a.at[o - 1],
+            device_id=(d, to), device_id_type=MESH)
+        first[o].start()
+    own = pltpu.make_async_copy(block_ref.at[t], out_ref.at[d, t], own_sem)
+    own.start()
+    turns = [0] + order
+    lag = 2
+    for i in range(len(turns) + lag):
+        if 0 < i < len(turns):
+            o = turns[i]
+            first[o].wait_recv()
+            outward(out_ref.at[d, lax.rem(t + owners - o, owners)], o)
+        if i >= lag:
+            onward(i - lag, turns[i - lag])
+    own.wait()
+    for o in order:
+        first[o].wait_send()
+    for i, o in enumerate(turns):
+        direct[o][1 - i % 2].wait_recv()
+        direct[o][0].wait_send()
+        direct[o][1].wait_send()
+    for copy in passed:
+        copy.wait()
+
+
 def spread(blocks, n_dp):
     owners, length, side = blocks.shape
     return pl.pallas_call(
-        functools.partial(spread_kernel, n_dp, owners),
+        functools.partial(square_kernel if n_dp == 4 else spread_kernel, n_dp, owners),
         out_shape=jax.ShapeDtypeStruct((n_dp, owners, length, side), blocks.dtype),
         in_specs=[pl.BlockSpec(memory_space=pl.ANY)],
         out_specs=pl.BlockSpec(memory_space=pl.ANY),

time: 216 us -> 202 us (0.935)
  Pallas kernels: 104 us -> 89.2 us
    pallas_call x1, Pallas kernels: 77.6 us -> 63.1 us  [spread(): pl.pallas_call(functools.partial(square_kernel if n_dp == 4 else spread_k...]
where the time goes in v3:
time: 202 us; the launch traced here: 201 us
  Pallas kernels  89.2 us (44%)
  waiting for transfers between devices  88.3 us (44%)
  between operations  14.1 us (7%)
  other arithmetic  5.57 us (3%)
  local copies, waits for them, and re-layouts  4.22 us (2%)
    reduce_scatter x1, waiting for transfers between devices, body(): total = lax.psum_scatter(parts, 'tensor', scatter_dimension=0, tiled=True)  88.3 us
    pallas_call x1, Pallas kernels, spread(): pl.pallas_call(functools.partial(square_kernel if n_dp == 4 else spread_k...  63.1 us
    pallas_call x1, Pallas kernels, local_pass(): pl.pallas_call(functools.partial(local_kernel, (rows, cols, owners, side,...  26.1 us
  transfers between devices with their start and end apart: 1, of which 1 were waited for; matrix products, arithmetic and copies ran while one was open for 0% of the time, Pallas kernels for 0%

profile of v3, /device:TPU:0, one launch (start us, length us, event | category | flops | bytes accessed | tf_op | source)
XLA Modules:
  0.0 201.4 jit_solution(14793930881629780819)
XLA Ops:
  7.2 0.0 reduce-scatter.2.cloned.1.call-start
  7.2 0.7 fusion
  7.9 0.7 fusion.2
  8.6 0.1 copy.13
  8.7 2.7 %pad_maximum_fusion.block_ref = bf16[8,784,128]{2,1,0:T(8,128)(2,1)} fusion(bf16[8,16,128]{2,1,0:T(8,128)(2,1)S(1)} %broadcast_in_dim.15, bf16[8,768,128]{2,1,0:T(8,128)(2,1)} %bitcast.12), kind=kLoop, calls=%fused_computation | loop fusion | flops 3211264 | bytes 3211264 | tf_op jit(solution)/shard_map/concatenate | solution.py:259
  11.4 63.1 %shard_map.68 = bf16[4,8,784,128]{3,2,1,0:T(8,128)(2,1)} custom-call(bf16[8,784,128]{2,1,0:T(8,128)(2,1)} %pad_maximum_fusion.block_ref), custom_call_target="tpu_custom_call" | custom-call | bytes 12845056 | tf_op jit(solution)/shard_map/pallas_call | solution.py:130
  74.5 0.9 slice_convert_fusion
  75.4 0.1 slice_compare_fusion
  75.4 0.1 fusion.4
  75.5 0.1 gt.11
  75.6 0.1 reshape.31.col_ref
  75.7 0.0 copy-start
  75.8 0.1 reshape.30.row_ref
  75.9 0.0 copy-start.1
  75.9 0.6 broadcast_select_fusion
  76.5 0.0 copy-done
  76.5 0.0 copy-done.1
  76.5 26.1 %shard_map.69 = bf16[8,2,8,256,128]{4,3,2,1,0:T(8,128)(2,1)} custom-call(s32[64]{0:T(128)} %copy-done.1, s32[64]{0:T(128)} %copy-done, s32[64]{0:T(128)} %get-tuple-element.11.row_to_ref, s32[64]{0:T(128)} %get-tuple-element.10.col_to_ref, bf16[256,8192]{1,0:T(8,128)(2,1)} %tok_ref.1, bf16[256,8192]{1,0:T(8,128)(2,1)} %grad_ref.1, bf16[32,784,128]{2,1,0:T(8,128)(2,1)} %bitcast.9), custom_call_target="tpu_custom_call" | custom-call | flops 3221225472 | bytes 31457280 | tf_op jit(solution)/shard_map/pallas_call | solution.py:221
  102.5 0.0 reduce-scatter.2.cloned.1.call-update
  102.6 88.3 %reduce-scatter.2.cloned.1.call-done = bf16[1,2,8,256,128]{4,3,2,1,0:T(8,128)(2,1)} async-done(((bf16[8,2,8,256,128]{4,3,2,1,0:T(8,128)(2,1)}), bf16[1,2,8,256,128]{4,3,2,1,0:T(8,128)(2,1)}) %reduce-scatter.2.cloned.1.call-update) | async-done | bytes 1048592 | tf_op jit(solution)/shard_map/reduce_scatter | solution.py:269
  190.9 1.3 fusion.3
  192.1 0.2 copy.10
  192.4 1.0 copy.12
  193.4 0.2 copy.9
  193.6 1.0 copy.11
  (3 shorter events, 0.0 us)
Async XLA Ops:
  7.2 183.7 %reduce-scatter.2.cloned.1.call-start = ((), (), s32[]{:S(2)}) async-start(), calls=%async_computation.1 | async-start | bytes 9437184 | tf_op jit(solution)/shard_map/reduce_scatter | solution.py:269
  75.7 0.7 copy-start
  75.9 0.6 copy-start.1
Sparse Core Ops, SparseCore 0:
  102.7 88.1 reduce-scatter.1

commit v4 on v3

--- a/solution.py
+++ b/solution.py
@@ -142,6 +142,143 @@
         compiler_params=pltpu.CompilerParams(collective_id=0, has_side_effects=True),
         cost_estimate=pl.CostEstimate(flops=0, bytes_accessed=2 * n_dp * blocks.size * 2, transcendentals=0),
     )(blocks)
+
+
+def line_kernel(chips, chunks, part_ref, out_ref, in_ref, mate_buf, sent, from_buf,
+                mate_send, mate_recv, line_send, line_recv):
+    d, t = lax.axis_index("dp"), lax.axis_index("tensor")
+    z, c = t // 2, lax.rem(t, 2)
+    owners, last = 2 * chips, chips - 1
+    mate = t + 1 - 2 * c
+    tiles = part_ref.shape[1]
+    size = tiles // chunks
+    half = tiles // 2
+    side = part_ref.shape[-1]
+    onward = (lax.rem(t + 2, owners), lax.rem(t + owners - 2, owners))
+    has_next = (z < last, z > 0)
+    has_before = (z > 0, z < last)
+
+    barrier = pltpu.get_barrier_semaphore()
+    pl.semaphore_signal(barrier, inc=1, device_id=(d, mate), device_id_type=MESH)
+    for way in range(2):
+        @pl.when(has_next[way])
+        def _():
+            pl.semaphore_signal(barrier, inc=1, device_id=(d, onward[way]), device_id_type=MESH)
+    inner = (z > 0) & (z < last)
+
+    @pl.when(inner)
+    def _():
+        pl.semaphore_wait(barrier, 3)
+
+    @pl.when(jnp.logical_not(inner))
+    def _():
+        pl.semaphore_wait(barrier, 2)
+
+    swaps = {}
+    order = []
+    for k in range(chips // 2):
+        order += [last - k, k]
+    for to in order:
+        swaps[to] = pltpu.make_async_remote_copy(
+            src_ref=part_ref.at[2 * to + 1 - c], dst_ref=mate_buf.at[to],
+            send_sem=mate_send.at[to], recv_sem=mate_recv.at[to],
+            device_id=(d, mate), device_id_type=MESH)
+        swaps[to].start()
+    for to in order:
+        swaps[to].wait_recv()
+
+    def hop(way, to, q):
+        at = pl.ds(q * size, size)
+        return pltpu.make_async_remote_copy(
+            src_ref=sent.at[to, at], dst_ref=from_buf.at[way, to, at],
+            send_sem=line_send.at[way, to, q], recv_sem=line_recv.at[way, to, q],
+            device_id=(d, onward[way]), device_id_type=MESH)
+
+    def own_sum(to, i):
+        return part_ref[2 * to + c, i].astype(F32) + mate_buf[to, i].astype(F32)
+
+    for k in range(last):
+        @pl.loop(0, chunks)
+        def _(q):
+            for way, to in ((0, last - k), (1, k)):
+                goes = (z < to) if way == 0 else (z > to)
+
+                @pl.when(goes & has_before[way])
+                def _():
+                    hop(way, to, q).wait_recv()
+                    for j in range(size):
+                        i = q * size + j
+                        sent[to, i] = (own_sum(to, i) + from_buf[way, to, i].astype(F32)).astype(jnp.bfloat16)
+                    hop(way, to, q).start()
+
+                @pl.when(goes & jnp.logical_not(has_before[way]))
+                def _():
+                    for j in range(size):
+                        i = q * size + j
+                        sent[to, i] = own_sum(to, i).astype(jnp.bfloat16)
+                    hop(way, to, q).start()
+
+    def finish(ways):
+        for q in range(chunks):
+            for way in ways:
+                hop(way, z, q).wait_recv()
+            for j in range(size):
+                i = q * size + j
+                total = own_sum(z, i)
+                for way in ways:
+                    total = total + from_buf[way, z, i].astype(F32)
+                to_ref = out_ref if i < half else in_ref
+                col = i % half * side
+                to_ref[:, col:col + side] = total.astype(jnp.bfloat16)
+
+    @pl.when(z == 0)
+    def _():
+        finish((1,))
+
+    @pl.when(z == last)
+    def _():
+        finish((0,))
+
+    @pl.when((z > 0) & (z < last))
+    def _():
+        finish((0, 1))
+
+    for to in order:
+        swaps[to].wait_send()
+    for k in range(last):
+        @pl.loop(0, chunks)
+        def _(q):
+            for way, to in ((0, last - k), (1, k)):
+                goes = (z < to) if way == 0 else (z > to)
+
+                @pl.when(goes)
+                def _():
+                    hop(way, to, q).wait_send()
+
+
+def line_sum(parts, chunks=4):
+    owners, _, per, toks, side = parts.shape
+    chips, tiles = owners // 2, 2 * per
+    parts = parts.reshape(owners, tiles, toks, side)
+    result = jax.ShapeDtypeStruct((toks, per * side), jnp.bfloat16)
+    vmem = pl.BlockSpec(memory_space=pltpu.VMEM)
+    return pl.pallas_call(
+        functools.partial(line_kernel, chips, chunks),
+        out_shape=(result, result),
+        in_specs=[vmem],
+        out_specs=(vmem, vmem),
+        scratch_shapes=[
+            pltpu.VMEM((chips, tiles, toks, side), jnp.bfloat16),
+            pltpu.VMEM((chips, tiles, toks, side), jnp.bfloat16),
+            pltpu.VMEM((2, chips, tiles, toks, side), jnp.bfloat16),
+            pltpu.SemaphoreType.DMA((chips,)),
+            pltpu.SemaphoreType.DMA((chips,)),
+            pltpu.SemaphoreType.DMA((2, chips, chunks)),
+            pltpu.SemaphoreType.DMA((2, chips, chunks)),
+        ],
+        compiler_params=pltpu.CompilerParams(collective_id=1, has_side_effects=True, vmem_limit_bytes=48 * 2**20),
+        cost_estimate=pl.CostEstimate(flops=parts.size, bytes_accessed=2 * parts.size, transcendentals=0),
+    )(parts)
 
 
 def tile_of(tile_ref, peer, j, g):
@@ -266,6 +403,8 @@
     row_to = jnp.where(live, row, rows)
     col_to = jnp.where(live, col, cols)
     parts = local_pass(tokens, out_grad, tiles, row, col, row_to, col_to, owners, cols, peer)
+    if (n_dp, owners) == (4, 8):
+        return line_sum(parts)
     total = lax.psum_scatter(parts, "tensor", scatter_dimension=0, tiled=True)
     total = jnp.transpose(total[0], (0, 2, 1, 3)).reshape(2, toks, feats // owners)
     return total[0], total[1]

time: 202 us -> 188 us (0.931)
  the two profiles are of different devices: /device:TPU:0 before, /device:TPU:10 now
where the time goes in v4:
time: 188 us
  Pallas kernels  179 us (95%)
  other arithmetic  5.57 us (3%)
  local copies, waits for them, and re-layouts  2.11 us (1%)
    pallas_call x1, Pallas kernels, line_sum(): pl.pallas_call(functools.partial(line_kernel, chips, chunks), out_shape=(...  93.8 us
    pallas_call x1, Pallas kernels, spread(): pl.pallas_call(functools.partial(square_kernel if n_dp == 4 else spread_k...  59.5 us
    pallas_call x1, Pallas kernels, local_pass(): pl.pallas_call(functools.partial(local_kernel, (rows, cols, owners, side,...  26.1 us

profile of v4, /device:TPU:10, one launch (start us, length us, event | category | flops | bytes accessed | tf_op | source)
XLA Modules:
  0.0 187.8 jit_solution(634246504715156862)
XLA Ops:
  0.6 0.7 fusion
  1.3 0.7 fusion.2
  2.0 0.1 copy.9
  2.1 2.7 %pad_maximum_fusion.block_ref = bf16[8,784,128]{2,1,0:T(8,128)(2,1)} fusion(bf16[8,16,128]{2,1,0:T(8,128)(2,1)S(1)} %broadcast_in_dim.15, bf16[8,768,128]{2,1,0:T(8,128)(2,1)} %bitcast.7), kind=kLoop, calls=%fused_computation | loop fusion | flops 3211264 | bytes 3211264 | tf_op jit(solution)/shard_map/concatenate | solution.py:396
  4.8 59.5 %shard_map.68 = bf16[4,8,784,128]{3,2,1,0:T(8,128)(2,1)} custom-call(bf16[8,784,128]{2,1,0:T(8,128)(2,1)} %pad_maximum_fusion.block_ref), custom_call_target="tpu_custom_call" | custom-call | bytes 12845056 | tf_op jit(solution)/shard_map/pallas_call | solution.py:130
  64.3 0.9 slice_convert_fusion
  65.2 0.1 slice_compare_fusion
  65.3 0.1 gt.11
  65.4 0.1 fusion.3
  65.5 0.1 reshape.29.col_ref
  65.6 0.0 copy-start
  65.6 0.1 reshape.28.row_ref
  65.7 0.0 copy-start.1
  65.7 0.6 broadcast_select_fusion
  66.3 0.0 copy-done
  66.3 0.0 copy-done.1
  66.3 26.1 %shard_map.69 = bf16[8,2,8,256,128]{4,3,2,1,0:T(8,128)(2,1)} custom-call(s32[64]{0:T(128)} %copy-done.1, s32[64]{0:T(128)} %copy-done, s32[64]{0:T(128)} %get-tuple-element.7.row_to_ref, s32[64]{0:T(128)} %get-tuple-element.6.col_to_ref, bf16[256,8192]{1,0:T(8,128)(2,1)} %tok_ref.1, bf16[256,8192]{1,0:T(8,128)(2,1)} %grad_ref.1, bf16[32,784,128]{2,1,0:T(8,128)(2,1)} %bitcast.6), custom_call_target="tpu_custom_call" | custom-call | flops 3221225472 | bytes 31457280 | tf_op jit(solution)/shard_map/pallas_call | solution.py:358
  92.4 93.8 %shard_map.70 = (bf16[256,1024]{1,0:T(8,128)(2,1)S(1)}, bf16[256,1024]{1,0:T(8,128)(2,1)S(1)}) custom-call(bf16[8,16,256,128]{3,2,1,0:T(8,128)(2,1)} %bitcast.4), custom_call_target="tpu_custom_call" | custom-call | flops 4194304 | bytes 8388608 | tf_op jit(solution)/shard_map/pallas_call | solution.py:265
  186.2 0.8 copy.12
  187.0 0.8 copy.13
  (3 shorter events, 0.0 us)
Async XLA Ops:
  65.6 0.7 copy-start
  65.7 0.6 copy-start.1

commit v5 on v4

--- a/solution.py
+++ b/solution.py
@@ -144,8 +144,8 @@
     )(blocks)
 
 
-def line_kernel(chips, chunks, part_ref, out_ref, in_ref, mate_buf, sent, from_buf,
-                mate_send, mate_recv, line_send, line_recv):
+def line_kernel(chips, chunks, part_ref, out_ref, in_ref, own_buf, mate_buf, sent, from_buf,
+                own_sem, mate_send, mate_recv, line_send, line_recv):
     d, t = lax.axis_index("dp"), lax.axis_index("tensor")
     z, c = t // 2, lax.rem(t, 2)
     owners, last = 2 * chips, chips - 1
@@ -174,7 +174,7 @@
     def _():
         pl.semaphore_wait(barrier, 2)
 
-    swaps = {}
+    swaps, loads = {}, {}
     order = []
     for k in range(chips // 2):
         order += [last - k, k]
@@ -184,8 +184,8 @@
             send_sem=mate_send.at[to], recv_sem=mate_recv.at[to],
             device_id=(d, mate), device_id_type=MESH)
         swaps[to].start()
-    for to in order:
-        swaps[to].wait_recv()
+        loads[to] = pltpu.make_async_copy(part_ref.at[2 * to + c], own_buf.at[to], own_sem.at[to])
+        loads[to].start()
 
     def hop(way, to, q):
         at = pl.ds(q * size, size)
@@ -195,9 +195,13 @@
             device_id=(d, onward[way]), device_id_type=MESH)
 
     def own_sum(to, i):
-        return part_ref[2 * to + c, i].astype(F32) + mate_buf[to, i].astype(F32)
+        return own_buf[to, i].astype(F32) + mate_buf[to, i].astype(F32)
 
     for k in range(last):
+        for to in order[2 * k:2 * k + 2]:
+            loads[to].wait()
+            swaps[to].wait_recv()
+
         @pl.loop(0, chunks)
         def _(q):
             for way, to in ((0, last - k), (1, k)):
@@ -265,18 +269,20 @@
     return pl.pallas_call(
         functools.partial(line_kernel, chips, chunks),
         out_shape=(result, result),
-        in_specs=[vmem],
+        in_specs=[pl.BlockSpec(memory_space=pl.ANY)],
         out_specs=(vmem, vmem),
         scratch_shapes=[
+            pltpu.VMEM((chips, tiles, toks, side), jnp.bfloat16),
             pltpu.VMEM((chips, tiles, toks, side), jnp.bfloat16),
             pltpu.VMEM((chips, tiles, toks, side), jnp.bfloat16),
             pltpu.VMEM((2, chips, tiles, toks, side), jnp.bfloat16),
             pltpu.SemaphoreType.DMA((chips,)),
             pltpu.SemaphoreType.DMA((chips,)),
+            pltpu.SemaphoreType.DMA((chips,)),
             pltpu.SemaphoreType.DMA((2, chips, chunks)),
             pltpu.SemaphoreType.DMA((2, chips, chunks)),
         ],
-        compiler_params=pltpu.CompilerParams(collective_id=1, has_side_effects=True, vmem_limit_bytes=48 * 2**20),
+        compiler_params=pltpu.CompilerParams(collective_id=1, has_side_effects=True, vmem_limit_bytes=58 * 2**20),
         cost_estimate=pl.CostEstimate(flops=parts.size, bytes_accessed=2 * parts.size, transcendentals=0),
     )(parts)
 

time: 188 us -> 185 us (0.984)
  Pallas kernels: 179 us -> 174 us
  local copies, waits for them, and re-layouts: 2.11 us -> 4.26 us
    pallas_call x1, Pallas kernels: 93.8 us -> 88.4 us  [line_sum(): pl.pallas_call(functools.partial(line_kernel, chips, chunks), out_shape=(...]
    unnamed x7, local copies, waits for them, and re-layouts: 1.7 us -> 3.84 us
where the time goes in v5:
time: 185 us
  Pallas kernels  174 us (94%)
  other arithmetic  5.57 us (3%)
  local copies, waits for them, and re-layouts  4.26 us (2%)
    pallas_call x1, Pallas kernels, line_sum(): pl.pallas_call(functools.partial(line_kernel, chips, chunks), out_shape=(...  88.4 us
    pallas_call x1, Pallas kernels, spread(): pl.pallas_call(functools.partial(square_kernel if n_dp == 4 else spread_k...  59.5 us
    pallas_call x1, Pallas kernels, local_pass(): pl.pallas_call(functools.partial(local_kernel, (rows, cols, owners, side,...  26.1 us
    unnamed x7, local copies, waits for them, and re-layouts  3.84 us

profile of v5, /device:TPU:10, one launch (start us, length us, event | category | flops | bytes accessed | tf_op | source)
XLA Modules:
  0.0 184.6 jit_solution(12968743203907212502)
XLA Ops:
  0.6 0.7 fusion
  1.3 0.7 fusion.2
  2.0 0.1 copy.9
  2.1 2.7 %pad_maximum_fusion.block_ref = bf16[8,784,128]{2,1,0:T(8,128)(2,1)} fusion(bf16[8,16,128]{2,1,0:T(8,128)(2,1)S(1)} %broadcast_in_dim.15, bf16[8,768,128]{2,1,0:T(8,128)(2,1)} %bitcast.7), kind=kLoop, calls=%fused_computation | loop fusion | flops 3211264 | bytes 3211264 | tf_op jit(solution)/shard_map/concatenate | solution.py:402
  4.8 59.5 %shard_map.68 = bf16[4,8,784,128]{3,2,1,0:T(8,128)(2,1)} custom-call(bf16[8,784,128]{2,1,0:T(8,128)(2,1)} %pad_maximum_fusion.block_ref), custom_call_target="tpu_custom_call" | custom-call | bytes 12845056 | tf_op jit(solution)/shard_map/pallas_call | solution.py:130
  64.3 0.9 slice_convert_fusion
  65.2 0.1 slice_compare_fusion
  65.3 0.1 gt.11
  65.4 0.1 fusion.3
  65.5 0.1 reshape.29.col_ref
  65.6 0.0 copy-start
  65.6 0.1 reshape.28.row_ref
  65.7 0.0 copy-start.1
  65.7 0.6 broadcast_select_fusion
  66.3 0.0 copy-done
  66.3 0.0 copy-done.1
  66.3 26.1 %shard_map.69 = bf16[8,2,8,256,128]{4,3,2,1,0:T(8,128)(2,1)} custom-call(s32[64]{0:T(128)} %copy-done.1, s32[64]{0:T(128)} %copy-done, s32[64]{0:T(128)} %get-tuple-element.7.row_to_ref, s32[64]{0:T(128)} %get-tuple-element.6.col_to_ref, bf16[256,8192]{1,0:T(8,128)(2,1)} %tok_ref.1, bf16[256,8192]{1,0:T(8,128)(2,1)} %grad_ref.1, bf16[32,784,128]{2,1,0:T(8,128)(2,1)} %bitcast.6), custom_call_target="tpu_custom_call" | custom-call | flops 3221225472 | bytes 31457280 | tf_op jit(solution)/shard_map/pallas_call | solution.py:364
  92.4 88.4 %shard_map.70 = (bf16[256,1024]{1,0:T(8,128)(2,1)}, bf16[256,1024]{1,0:T(8,128)(2,1)}) custom-call(bf16[8,16,256,128]{3,2,1,0:T(8,128)(2,1)} %bitcast.4), custom_call_target="tpu_custom_call" | custom-call | flops 4194304 | bytes 8388608 | tf_op jit(solution)/shard_map/pallas_call | solution.py:269
  180.8 1.9 %copy.12 = bf16[256,1024]{1,0:T(8,128)(2,1)} copy(bf16[256,1024]{1,0:T(8,128)(2,1)} %get-tuple-element.10) | data formatting | bytes 1048576
  182.7 1.9 %copy.13 = bf16[256,1024]{1,0:T(8,128)(2,1)} copy(bf16[256,1024]{1,0:T(8,128)(2,1)} %get-tuple-element.11) | data formatting | bytes 1048576
  (3 shorter events, 0.0 us)
Async XLA Ops:
  65.6 0.7 copy-start
  65.7 0.6 copy-start.1

commit v6 on v5

--- a/solution.py
+++ b/solution.py
@@ -260,7 +260,7 @@
                     hop(way, to, q).wait_send()
 
 
-def line_sum(parts, chunks=4):
+def line_sum(parts, chunks=8):
     owners, _, per, toks, side = parts.shape
     chips, tiles = owners // 2, 2 * per
     parts = parts.reshape(owners, tiles, toks, side)

time: 185 us -> 197 us (1.065); the launches traced: 185 us -> 194 us
  Pallas kernels: 174 us -> 184 us
    pallas_call x1, Pallas kernels: 88.4 us -> 98.3 us  [line_sum(): pl.pallas_call(functools.partial(line_kernel, chips, chunks), out_shape=(...]
where the time goes in v6:
time: 197 us; the launch traced here: 194 us
  Pallas kernels  184 us (93%)
  other arithmetic  5.57 us (3%)
  local copies, waits for them, and re-layouts  4.26 us (2%)
    pallas_call x1, Pallas kernels, line_sum(): pl.pallas_call(functools.partial(line_kernel, chips, chunks), out_shape=(...  98.3 us
    pallas_call x1, Pallas kernels, spread(): pl.pallas_call(functools.partial(square_kernel if n_dp == 4 else spread_k...  59.5 us
    pallas_call x1, Pallas kernels, local_pass(): pl.pallas_call(functools.partial(local_kernel, (rows, cols, owners, side,...  26 us

profile of v6, /device:TPU:10, one launch (start us, length us, event | category | flops | bytes accessed | tf_op | source)
XLA Modules:
  0.0 194.4 jit_solution(16057665860667865911)
XLA Ops:
  0.6 0.7 fusion
  1.3 0.7 fusion.2
  2.0 0.1 copy.9
  2.1 2.7 %pad_maximum_fusion.block_ref = bf16[8,784,128]{2,1,0:T(8,128)(2,1)} fusion(bf16[8,16,128]{2,1,0:T(8,128)(2,1)S(1)} %broadcast_in_dim.15, bf16[8,768,128]{2,1,0:T(8,128)(2,1)} %bitcast.7), kind=kLoop, calls=%fused_computation | loop fusion | flops 3211264 | bytes 3211264 | tf_op jit(solution)/shard_map/concatenate | solution.py:402
  4.8 59.5 %shard_map.68 = bf16[4,8,784,128]{3,2,1,0:T(8,128)(2,1)} custom-call(bf16[8,784,128]{2,1,0:T(8,128)(2,1)} %pad_maximum_fusion.block_ref), custom_call_target="tpu_custom_call" | custom-call | bytes 12845056 | tf_op jit(solution)/shard_map/pallas_call | solution.py:130
  64.3 0.9 slice_convert_fusion
  65.2 0.1 slice_compare_fusion
  65.3 0.1 gt.11
  65.4 0.1 fusion.3
  65.5 0.1 reshape.29.col_ref
  65.6 0.0 copy-start
  65.6 0.1 reshape.28.row_ref
  65.7 0.0 copy-start.1
  65.7 0.6 broadcast_select_fusion
  66.3 0.0 copy-done
  66.3 0.0 copy-done.1
  66.3 26.0 %shard_map.69 = bf16[8,2,8,256,128]{4,3,2,1,0:T(8,128)(2,1)} custom-call(s32[64]{0:T(128)} %copy-done.1, s32[64]{0:T(128)} %copy-done, s32[64]{0:T(128)} %get-tuple-element.7.row_to_ref, s32[64]{0:T(128)} %get-tuple-element.6.col_to_ref, bf16[256,8192]{1,0:T(8,128)(2,1)} %tok_ref.1, bf16[256,8192]{1,0:T(8,128)(2,1)} %grad_ref.1, bf16[32,784,128]{2,1,0:T(8,128)(2,1)} %bitcast.6), custom_call_target="tpu_custom_call" | custom-call | flops 3221225472 | bytes 31457280 | tf_op jit(solution)/shard_map/pallas_call | solution.py:364
  92.4 98.3 %shard_map.70 = (bf16[256,1024]{1,0:T(8,128)(2,1)}, bf16[256,1024]{1,0:T(8,128)(2,1)}) custom-call(bf16[8,16,256,128]{3,2,1,0:T(8,128)(2,1)} %bitcast.4), custom_call_target="tpu_custom_call" | custom-call | flops 4194304 | bytes 8388608 | tf_op jit(solution)/shard_map/pallas_call | solution.py:269
  190.6 1.9 copy.12
  192.5 1.9 copy.13
  (3 shorter events, 0.0 us)
Async XLA Ops:
  65.6 0.7 copy-start
  65.7 0.6 copy-start.1

commit v7 on v5

--- a/solution.py
+++ b/solution.py
@@ -8,7 +8,7 @@
 from jax.sharding import PartitionSpec as P
 
 FF = 26624
-GROUP = 8
+GROUP = 16
 F32 = jnp.float32
 NT = (((1,), (1,)), ((), ()))
 MESH = pl.DeviceIdType.MESH

time: 185 us -> 181 us (0.978)
  Pallas kernels: 174 us -> 170 us
    pallas_call x1, Pallas kernels: 26.1 us -> 22.1 us  [local_pass(): pl.pallas_call(functools.partial(local_kernel, (rows, cols, owners, side,...]
where the time goes in v7:
time: 181 us
  Pallas kernels  170 us (94%)
  other arithmetic  5.57 us (3%)
  local copies, waits for them, and re-layouts  4.26 us (2%)
    pallas_call x1, Pallas kernels, line_sum(): pl.pallas_call(functools.partial(line_kernel, chips, chunks), out_shape=(...  88.5 us
    pallas_call x1, Pallas kernels, spread(): pl.pallas_call(functools.partial(square_kernel if n_dp == 4 else spread_k...  59.5 us
    pallas_call x1, Pallas kernels, local_pass(): pl.pallas_call(functools.partial(local_kernel, (rows, cols, owners, side,...  22.1 us
    unnamed x7, local copies, waits for them, and re-layouts  3.84 us

profile of v7, /device:TPU:10, one launch (start us, length us, event | category | flops | bytes accessed | tf_op | source)
XLA Modules:
  0.0 180.7 jit_solution(16297375643463753844)
XLA Ops:
  0.6 0.7 fusion
  1.3 0.7 fusion.2
  2.0 0.1 copy.9
  2.1 2.7 %pad_maximum_fusion.block_ref = bf16[8,784,128]{2,1,0:T(8,128)(2,1)} fusion(bf16[8,16,128]{2,1,0:T(8,128)(2,1)S(1)} %broadcast_in_dim.15, bf16[8,768,128]{2,1,0:T(8,128)(2,1)} %bitcast.7), kind=kLoop, calls=%fused_computation | loop fusion | flops 3211264 | bytes 3211264 | tf_op jit(solution)/shard_map/concatenate | solution.py:402
  4.8 59.5 %shard_map.68 = bf16[4,8,784,128]{3,2,1,0:T(8,128)(2,1)} custom-call(bf16[8,784,128]{2,1,0:T(8,128)(2,1)} %pad_maximum_fusion.block_ref), custom_call_target="tpu_custom_call" | custom-call | bytes 12845056 | tf_op jit(solution)/shard_map/pallas_call | solution.py:130
  64.3 0.9 slice_convert_fusion
  65.2 0.1 slice_compare_fusion
  65.3 0.1 gt.11
  65.4 0.1 fusion.3
  65.5 0.1 reshape.29.col_ref
  65.6 0.0 copy-start
  65.6 0.1 reshape.28.row_ref
  65.7 0.0 copy-start.1
  65.7 0.6 broadcast_select_fusion
  66.3 0.0 copy-done
  66.3 0.0 copy-done.1
  66.3 22.1 %shard_map.69 = bf16[8,2,8,256,128]{4,3,2,1,0:T(8,128)(2,1)} custom-call(s32[64]{0:T(128)} %copy-done.1, s32[64]{0:T(128)} %copy-done, s32[64]{0:T(128)} %get-tuple-element.7.row_to_ref, s32[64]{0:T(128)} %get-tuple-element.6.col_to_ref, bf16[256,8192]{1,0:T(8,128)(2,1)} %tok_ref.1, bf16[256,8192]{1,0:T(8,128)(2,1)} %grad_ref.1, bf16[32,784,128]{2,1,0:T(8,128)(2,1)} %bitcast.6), custom_call_target="tpu_custom_call" | custom-call | flops 3221225472 | bytes 31457280 | tf_op jit(solution)/shard_map/pallas_call | solution.py:364
  88.4 88.5 %shard_map.70 = (bf16[256,1024]{1,0:T(8,128)(2,1)}, bf16[256,1024]{1,0:T(8,128)(2,1)}) custom-call(bf16[8,16,256,128]{3,2,1,0:T(8,128)(2,1)} %bitcast.4), custom_call_target="tpu_custom_call" | custom-call | flops 4194304 | bytes 8388608 | tf_op jit(solution)/shard_map/pallas_call | solution.py:269
  177.0 1.9 %copy.12 = bf16[256,1024]{1,0:T(8,128)(2,1)} copy(bf16[256,1024]{1,0:T(8,128)(2,1)} %get-tuple-element.10) | data formatting | bytes 1048576
  178.8 1.9 %copy.13 = bf16[256,1024]{1,0:T(8,128)(2,1)} copy(bf16[256,1024]{1,0:T(8,128)(2,1)} %get-tuple-element.11) | data formatting | bytes 1048576
  (3 shorter events, 0.0 us)
Async XLA Ops:
  65.6 0.7 copy-start
  65.7 0.6 copy-start.1

commit v8 on v7

--- a/solution.py
+++ b/solution.py
@@ -260,7 +260,7 @@
                     hop(way, to, q).wait_send()
 
 
-def line_sum(parts, chunks=4):
+def line_sum(parts, chunks=2):
     owners, _, per, toks, side = parts.shape
     chips, tiles = owners // 2, 2 * per
     parts = parts.reshape(owners, tiles, toks, side)

time: 181 us -> 188 us (1.039)
  Pallas kernels: 170 us -> 177 us
    pallas_call x1, Pallas kernels: 88.5 us -> 95.5 us  [line_sum(): pl.pallas_call(functools.partial(line_kernel, chips, chunks), out_shape=(...]
where the time goes in v8:
time: 188 us
  Pallas kernels  177 us (94%)
  other arithmetic  5.57 us (3%)
  local copies, waits for them, and re-layouts  4.26 us (2%)
    pallas_call x1, Pallas kernels, line_sum(): pl.pallas_call(functools.partial(line_kernel, chips, chunks), out_shape=(...  95.5 us
    pallas_call x1, Pallas kernels, spread(): pl.pallas_call(functools.partial(square_kernel if n_dp == 4 else spread_k...  59.5 us
    pallas_call x1, Pallas kernels, local_pass(): pl.pallas_call(functools.partial(local_kernel, (rows, cols, owners, side,...  22.1 us
    unnamed x7, local copies, waits for them, and re-layouts  3.84 us

profile of v8, /device:TPU:10, one launch (start us, length us, event | category | flops | bytes accessed | tf_op | source)
XLA Modules:
  0.0 187.6 jit_solution(4312109332896482845)
XLA Ops:
  0.6 0.7 fusion
  1.3 0.7 fusion.2
  2.0 0.1 copy.9
  2.1 2.7 %pad_maximum_fusion.block_ref = bf16[8,784,128]{2,1,0:T(8,128)(2,1)} fusion(bf16[8,16,128]{2,1,0:T(8,128)(2,1)S(1)} %broadcast_in_dim.15, bf16[8,768,128]{2,1,0:T(8,128)(2,1)} %bitcast.7), kind=kLoop, calls=%fused_computation | loop fusion | flops 3211264 | bytes 3211264 | tf_op jit(solution)/shard_map/concatenate | solution.py:402
  4.8 59.5 %shard_map.68 = bf16[4,8,784,128]{3,2,1,0:T(8,128)(2,1)} custom-call(bf16[8,784,128]{2,1,0:T(8,128)(2,1)} %pad_maximum_fusion.block_ref), custom_call_target="tpu_custom_call" | custom-call | bytes 12845056 | tf_op jit(solution)/shard_map/pallas_call | solution.py:130
  64.3 0.9 slice_convert_fusion
  65.2 0.1 slice_compare_fusion
  65.3 0.1 gt.11
  65.4 0.1 fusion.3
  65.5 0.1 reshape.29.col_ref
  65.6 0.0 copy-start
  65.6 0.1 reshape.28.row_ref
  65.7 0.0 copy-start.1
  65.7 0.6 broadcast_select_fusion
  66.3 0.0 copy-done
  66.3 0.0 copy-done.1
  66.3 22.1 %shard_map.69 = bf16[8,2,8,256,128]{4,3,2,1,0:T(8,128)(2,1)} custom-call(s32[64]{0:T(128)} %copy-done.1, s32[64]{0:T(128)} %copy-done, s32[64]{0:T(128)} %get-tuple-element.7.row_to_ref, s32[64]{0:T(128)} %get-tuple-element.6.col_to_ref, bf16[256,8192]{1,0:T(8,128)(2,1)} %tok_ref.1, bf16[256,8192]{1,0:T(8,128)(2,1)} %grad_ref.1, bf16[32,784,128]{2,1,0:T(8,128)(2,1)} %bitcast.6), custom_call_target="tpu_custom_call" | custom-call | flops 3221225472 | bytes 31457280 | tf_op jit(solution)/shard_map/pallas_call | solution.py:364
  88.4 95.5 %shard_map.70 = (bf16[256,1024]{1,0:T(8,128)(2,1)}, bf16[256,1024]{1,0:T(8,128)(2,1)}) custom-call(bf16[8,16,256,128]{3,2,1,0:T(8,128)(2,1)} %bitcast.4), custom_call_target="tpu_custom_call" | custom-call | flops 4194304 | bytes 8388608 | tf_op jit(solution)/shard_map/pallas_call | solution.py:269
  183.9 1.9 copy.12
  185.8 1.9 copy.13
  (3 shorter events, 0.0 us)
Async XLA Ops:
  65.6 0.7 copy-start
  65.7 0.6 copy-start.1
